TPU v7x, 512 devices: a whole 4x8x8 slice. The times are simulated.
512 devices in a mesh: ctx: 32 (over x, y), tp: 16 (over z, core).
Axes of the slice: x: 4, y: 8, z: 8, core: 2. Of those that a mesh axis runs over, the one named last changes fastest.
Arguments:
- prefix_x: bfloat16 [8192, 8192], P('ctx', 'tp'), may hold values from -6 to 6
- prefix_z: bfloat16 [8192, 8192], P('ctx', 'tp'), may hold values from -6 to 6
- prefix_bc: bfloat16 [8192, 256], P(('ctx', 'tp')), may hold values from -6 to 6
- prefix_dt: float32 [128, 8192], P('tp', 'ctx'), may hold values from -6 to 6
- branch_x: bfloat16 [8192, 8192], P('ctx', 'tp'), may hold values from -6 to 6
- branch_z: bfloat16 [8192, 8192], P('ctx', 'tp'), may hold values from -6 to 6
- branch_bc: bfloat16 [8192, 256], P(('ctx', 'tp')), may hold values from -6 to 6
- branch_dt: float32 [128, 8192], P('tp', 'ctx'), may hold values from -6 to 6
- conv_x: bfloat16 [4, 8192], P(None, 'tp'), may hold values from -3 to 3
- conv_bc: bfloat16 [4, 256], replicated, may hold values from -3 to 3
- decay_rate: float32 [128], P('tp'), may hold values from 2.4414063e-05 to 0.03
- skip: float32 [128], P('tp'), may hold values from 0.5 to 1.5
- norm_gain: float32 [8192], P('tp'), may hold values from 0.5 to 1.5
- bound_pos: int32 [8], replicated, may hold values from 0 to 8191
- branch_owner: int32 [64], replicated, may hold values from 0 to 31, as said below
- branch_parent: int32 [64], replicated, may hold values from 0 to 7
- branch_len: int32 [64], replicated, may hold values from 1 to 255, as said below
Outputs:
- prefix_out: bfloat16 [8192, 8192], P('ctx', 'tp')
- branch_out: bfloat16 [8192, 8192], P('ctx', 'tp')
Inputs may be any that keep to these rules, and one draw needn't show every extreme that they name: `branch_owner`: every block index 0 to 31 holds exactly 2 branches. `branch_len`: the branches of one block have lengths that sum to at most 256; in every draw some block's sum is exactly 256, and some branch has exactly 255 rows.
All inputs are finite; a program needn't handle non-finite values.
Results may differ from a plain program's by a relative error of at most 0.0034.
Values may be sent and summed in bfloat16 or wider, within the bound.
No kernel may reach another device: no remote copies, remote signals or barrier semaphores. Data moves between devices by JAX's collectives and lax.ppermute only.
A program may use at most 64 MiB of HBM per device.

v0:
```python
import jax
import jax.numpy as jnp
from jax import lax
from jax.sharding import PartitionSpec as P

NORM_GROUP = 8192
BR_PER = 2
EPSILON = 1e-05


def passed_along(value, axis, steps):
    count = lax.axis_size(axis)
    first, last = (max(0, -steps), min(count, count - steps))
    return lax.ppermute(value, axis, [(source, source + steps) for source in range(first, last)])


def conv_silu(lagged, weights):
    summed = weights[0].astype(jnp.float32)[None, :] * lagged[0].astype(jnp.float32)
    for tap_index in range(1, len(lagged)):
        summed = summed + weights[tap_index].astype(jnp.float32)[None, :] * lagged[
            tap_index
        ].astype(jnp.float32)
    return jax.nn.silu(summed).astype(jnp.bfloat16)


def split_conv(convolved, channels, head_count):
    length = convolved.shape[0]
    state_size = (convolved.shape[1] - channels) // 2
    values = convolved[:, :channels].reshape(length, head_count, channels // head_count)
    return (
        values,
        convolved[:, channels : channels + state_size],
        convolved[:, channels + state_size :],
    )


def decays(raw_steps, rates):
    step_size = jax.nn.softplus(raw_steps)
    log_decay = -rates[:, None] * step_size
    return (step_size, log_decay, jnp.cumsum(log_decay, axis=1))


def intra_block(values, b_rows, c_rows, step_size, cumulative, causal_mask):
    scores = jnp.dot(c_rows, b_rows.T, preferred_element_type=jnp.float32)
    exponent = jnp.where(causal_mask[None], cumulative[:, :, None] - cumulative[:, None, :], 0.0)
    mixing = jnp.where(
        causal_mask[None], scores[None] * jnp.exp(exponent) * step_size[:, None, :], 0.0
    ).astype(jnp.bfloat16)
    return jnp.einsum("hts,shp->thp", mixing, values, preferred_element_type=jnp.float32)


def local_states(values, b_rows, step_size, cumulative, positions):
    length = cumulative.shape[1]
    clipped = jnp.clip(positions, 0, length - 1)
    decay_end = jnp.take(cumulative, clipped, axis=1)
    row_index = jnp.arange(length, dtype=jnp.int32)
    inside = row_index[None, :] <= positions[:, None]
    exponent = jnp.where(inside[:, None, :], decay_end.T[:, :, None] - cumulative[None], 0.0)
    weight = jnp.where(inside[:, None, :], jnp.exp(exponent) * step_size[None], 0.0)
    weighted = (
        jnp.transpose(weight, (0, 2, 1))[:, :, :, None] * values[None].astype(jnp.float32)
    ).astype(jnp.bfloat16)
    return jnp.einsum("jshp,sn->jhpn", weighted, b_rows, preferred_element_type=jnp.float32)


def from_state(c_rows, state, weight):
    result = jnp.einsum(
        "tn,hpn->thp", c_rows.astype(jnp.float32), state, precision=lax.Precision.HIGHEST
    )
    return result * weight.T[:, :, None]


def finish(mixed_out, values, skip, gate_rows, gain):
    length = mixed_out.shape[0]
    mixed_out = mixed_out + skip[None, :, None] * values.astype(jnp.float32)
    gated = mixed_out.reshape(length, -1) * jax.nn.silu(gate_rows.astype(jnp.float32))
    partial_squares = jnp.sum(gated * gated, axis=1, keepdims=True)
    total_squares = lax.psum(partial_squares, "tp")
    factor = lax.rsqrt(total_squares / NORM_GROUP + EPSILON)
    return (gated * factor * gain[None, :]).astype(jnp.bfloat16)


def layout(owner_index, branch_owner, branch_parent, branch_len, length):
    owned = (branch_owner == owner_index).astype(jnp.int32)
    owned_rank = jnp.cumsum(owned) - 1
    owned_lengths = owned * branch_len
    starts = jnp.cumsum(owned_lengths) - owned_lengths
    branch_slot = jnp.arange(BR_PER, dtype=jnp.int32)
    chosen = owned[None, :] * (owned_rank[None, :] == branch_slot[:, None]).astype(jnp.int32)
    segment_length = jnp.sum(chosen * branch_len[None, :], axis=1)
    segment_start = jnp.sum(chosen * starts[None, :], axis=1)
    parents = jnp.sum(chosen * branch_parent[None, :], axis=1)
    row_index = jnp.arange(length, dtype=jnp.int32)
    inside = (
        (row_index[None, :] >= segment_start[:, None])
        & (row_index[None, :] < (segment_start + segment_length)[:, None])
    ).astype(jnp.int32)
    live_count = jnp.sum(inside, axis=0)
    segment = jnp.sum(inside * branch_slot[:, None], axis=0) + BR_PER * (1 - live_count)
    offset = row_index - jnp.sum(inside * segment_start[:, None], axis=0)
    return (segment, offset, live_count > 0, parents)


def branch_block(
    joined_rows,
    gate_rows,
    raw_steps,
    all_states,
    all_tails,
    weights,
    rates,
    skip,
    gain,
    owner_index,
    branch_owner,
    branch_parent,
    branch_len,
):
    length, row_width = joined_rows.shape
    channels = gate_rows.shape[1]
    head_count = rates.shape[0]
    tail_count = weights.shape[0] - 1
    segment, offset, live_rows, parents = layout(
        owner_index, branch_owner, branch_parent, branch_len, length
    )
    seed_states = jnp.take(all_states, parents, axis=0)
    tail_rows = jnp.take(all_tails, parents, axis=0).reshape(-1, row_width).astype(jnp.bfloat16)
    column = jnp.arange(tail_rows.shape[0], dtype=jnp.int32)
    column_segment = column // tail_count
    column_row = column % tail_count
    lagged = []
    for tap_index in range(tail_count + 1):
        shift_rows = tail_count - tap_index
        if shift_rows == 0:
            lagged.append(joined_rows)
        else:
            shifted = jnp.concatenate(
                [
                    jnp.zeros((shift_rows, row_width), jnp.bfloat16),
                    joined_rows[: length - shift_rows],
                ],
                axis=0,
            )
            local_rows = jnp.where(
                (offset >= shift_rows)[:, None], shifted, jnp.zeros_like(shifted)
            )
            picker = (
                (segment[:, None] == column_segment[None, :])
                & (offset[:, None] < shift_rows)
                & (column_row[None, :] == tail_count - shift_rows + offset[:, None])
            ).astype(jnp.bfloat16)
            tail_part = jnp.dot(picker, tail_rows, preferred_element_type=jnp.float32).astype(
                jnp.bfloat16
            )
            lagged.append(local_rows + tail_part)
    values, b_rows, c_rows = split_conv(conv_silu(lagged, weights), channels, head_count)
    step_size, log_decay, cumulative = decays(raw_steps, rates)
    row_index = jnp.arange(length, dtype=jnp.int32)
    causal_mask = (
        (segment[:, None] == segment[None, :])
        & live_rows[:, None]
        & (row_index[None, :] <= row_index[:, None])
    )
    mixed_out = intra_block(values, b_rows, c_rows, step_size, cumulative, causal_mask)
    first_rows = jnp.clip(row_index - offset, 0, length - 1)
    start_log = jnp.take(cumulative - log_decay, first_rows, axis=1)
    seed_weight = jnp.where(
        live_rows[None, :], jnp.exp(jnp.where(live_rows[None, :], cumulative - start_log, 0.0)), 0.0
    )
    for branch_slot in range(seed_states.shape[0]):
        portion = from_state(c_rows, seed_states[branch_slot], seed_weight)
        mixed_out = mixed_out + jnp.where((segment == branch_slot)[:, None, None], portion, 0.0)
    result = finish(mixed_out, values, skip, gate_rows, gain)
    return jnp.where(live_rows[:, None], result, jnp.zeros_like(result))


def body(
    prefix_x,
    prefix_z,
    prefix_bc,
    prefix_dt,
    branch_x,
    branch_z,
    branch_bc,
    branch_dt,
    conv_x,
    conv_bc,
    decay_rate,
    skip,
    norm_gain,
    bound_pos,
    branch_owner,
    branch_parent,
    branch_len,
):
    prefix_gathered, branch_gathered = (
        lax.all_gather(prefix_bc, "tp", axis=0, tiled=True),
        lax.all_gather(branch_bc, "tp", axis=0, tiled=True),
    )
    length = prefix_x.shape[0]
    channels = prefix_x.shape[1]
    head_count = decay_rate.shape[0]
    weights = jnp.concatenate([conv_x, conv_bc], axis=1)
    tail_count = weights.shape[0] - 1
    joined_rows = jnp.concatenate([prefix_x, prefix_gathered], axis=1)
    before = passed_along(joined_rows[length - tail_count :], "ctx", 1)
    extended = jnp.concatenate([before, joined_rows], axis=0)
    lagged = [extended[tap_index : tap_index + length] for tap_index in range(tail_count + 1)]
    values, b_rows, c_rows = split_conv(conv_silu(lagged, weights), channels, head_count)
    step_size, log_decay, cumulative = decays(prefix_dt, decay_rate)
    row_index = jnp.arange(length, dtype=jnp.int32)
    causal_mask = row_index[None, :] <= row_index[:, None]
    mixed_out = intra_block(values, b_rows, c_rows, step_size, cumulative, causal_mask)
    owner_index = lax.axis_index("ctx")
    local_at = jnp.where(bound_pos // length == owner_index, bound_pos - owner_index * length, -1)
    positions = jnp.concatenate([local_at, jnp.full((1,), length - 1, jnp.int32)])
    states = local_states(values, b_rows, step_size, cumulative, positions)
    bound_count = bound_pos.shape[0]
    end_state = states[bound_count]
    end_decay = jnp.exp(cumulative[:, -1])

    def carry_step(unused, state):
        return passed_along(end_decay[:, None, None] * state + end_state, "ctx", 1)

    entering = lax.fori_loop(0, lax.axis_size("ctx") - 1, carry_step, jnp.zeros_like(end_state))
    mixed_out = mixed_out + from_state(c_rows, entering, jnp.exp(cumulative))
    prefix_out = finish(mixed_out, values, skip, prefix_z, norm_gain)
    held_here = local_at >= 0
    decay_at = jnp.exp(jnp.take(cumulative, jnp.clip(local_at, 0, length - 1), axis=1))
    candidate = jnp.where(
        held_here[:, None, None, None],
        decay_at.T[:, :, None, None] * entering[None] + states[:bound_count],
        0.0,
    )
    tail_index = (local_at[:, None] + 1 + jnp.arange(tail_count, dtype=jnp.int32)[None, :]).reshape(
        -1
    )
    held_rows = jnp.repeat(held_here, tail_count)
    picker = (
        (jnp.arange(length + tail_count, dtype=jnp.int32)[None, :] == tail_index[:, None])
        & held_rows[:, None]
    ).astype(jnp.bfloat16)
    tail_rows = jnp.dot(picker, extended, preferred_element_type=jnp.float32).reshape(
        bound_count, tail_count, -1
    )
    all_states, all_tails = lax.psum((candidate, tail_rows), "ctx")
    branch_joined = jnp.concatenate([branch_x, branch_gathered], axis=1)
    branch_out = branch_block(
        branch_joined,
        branch_z,
        branch_dt,
        all_states,
        all_tails,
        weights,
        decay_rate,
        skip,
        norm_gain,
        owner_index,
        branch_owner,
        branch_parent,
        branch_len,
    )
    return (prefix_out, branch_out)


def solution(mesh):
    in_specs = (
        P("ctx", "tp"),
        P("ctx", "tp"),
        P(("ctx", "tp"), None),
        P("tp", "ctx"),
        P("ctx", "tp"),
        P("ctx", "tp"),
        P(("ctx", "tp"), None),
        P("tp", "ctx"),
        P(None, "tp"),
        P(),
        P("tp"),
        P("tp"),
        P("tp"),
        P(),
        P(),
        P(),
        P(),
    )
    out_specs = (P("ctx", "tp"), P("ctx", "tp"))
    return jax.shard_map(body, mesh=mesh, in_specs=in_specs, out_specs=out_specs, check_vma=False)
```

profile of v0, /device:TPU:1, one launch (start us, length us, event | category | flops | bytes accessed | tf_op | source)
XLA Modules:
  0.0 639.3 jit_solution(6690966973142288056)
XLA Ops:
  8.3 25.1 %all_gather.6 = bf16[256,256]{1,0:T(8,128)(2,1)S(1)} all-gather(bf16[16,256]{1,0:T(8,128)(2,1)} %param.21), channel_id=1, replica_groups=mesh['ctx'=32,'tp'=16] {'tp'}, dimensions={0}, use_global_device_ids=true | all-gather | bytes 139264 | tf_op jit(solution)/shard_map/all_gather | solution.py:197
  50.8 14.8 %all_gather.7 = bf16[256,256]{1,0:T(8,128)(2,1)S(1)} all-gather(bf16[16,256]{1,0:T(8,128)(2,1)S(1)} %copy-done.27), channel_id=1, replica_groups=mesh['ctx'=32,'tp'=16] {'tp'}, dimensions={0}, use_global_device_ids=true | all-gather | bytes 139264 | tf_op jit(solution)/shard_map/all_gather | solution.py:198
  74.3 305.5 %while.10 = (s32[]{:T(128)}, f32[8,64,128]{2,1,0:T(8,128)S(1)}, f32[8]{0:T(128)}, f32[8,64,128]{2,1,0:T(8,128)S(1)}, s32[]{:T(128)}) while((s32[]{:T(128)}, f32[8,64,128]{2,1,0:T(8,128)S(1)}, f32[8]{0:T(128)}, f32[8,64,128]{2,1,0:T(8,128)S(1)}, s32[]{:T(128)}) %tuple.49), condition=%wide.region_3.4_spmd, body=%wide.region_2.3_spmd.sunk | while | flops 131074 | bytes 1835141 | solution.py:225
  78.2 5.5 collective-permute-done
  84.4 4.1 collective-permute-start
  88.6 4.6 collective-permute-done
  93.9 4.1 collective-permute-start
  98.0 3.7 collective-permute-done
  102.4 4.1 collective-permute-start
  106.5 3.3 collective-permute-done
  110.5 3.8 collective-permute-start
  114.3 3.3 collective-permute-done
  118.3 4.4 collective-permute-start
  122.8 3.3 collective-permute-done
  126.8 5.3 collective-permute-start
  132.1 3.3 collective-permute-done
  136.1 5.0 collective-permute-start
  141.1 3.3 collective-permute-done
  145.1 5.0 collective-permute-start
  150.2 4.0 collective-permute-done
  154.9 5.5 collective-permute-start
  160.3 5.0 collective-permute-done
  166.1 5.9 collective-permute-start
  172.0 6.0 collective-permute-done
  178.7 5.4 collective-permute-start
  184.0 4.8 collective-permute-done
  189.5 5.1 collective-permute-start
  194.6 3.7 collective-permute-done
  199.0 4.2 collective-permute-start
  203.2 3.3 collective-permute-done
  207.2 5.3 collective-permute-start
  216.5 5.3 collective-permute-start
  221.9 3.3 collective-permute-done
  225.8 5.5 collective-permute-start
  235.3 5.0 collective-permute-start
  240.3 3.3 collective-permute-done
  244.3 5.2 collective-permute-start
  249.5 4.2 collective-permute-done
  254.5 5.3 collective-permute-start
  259.8 5.0 collective-permute-done
  265.5 4.3 collective-permute-start
  269.9 5.6 collective-permute-done
  276.2 4.1 collective-permute-start
  280.4 5.7 collective-permute-done
  286.7 5.1 collective-permute-start
  291.9 5.8 collective-permute-done
  298.4 6.9 %collective-permute-start = (f32[8,64,128]{2,1,0:T(8,128)S(1)}, f32[8,64,128]{2,1,0:T(8,128)S(1)}, u32[]{:S(2)}, u32[]{:S(2)}) collective-permute-start(f32[8,64,128]{2,1,0:T(8,128)S(1)} %multiply_add_fusion.4), channel_id=1, source_target_pairs={{0,16},{16,32},{32,48},{48,64},{64,80},{80,96},{96,112},{112,128},... | collective-permute-start | bytes 786440 | tf_op jit(solution)/shard_map/while/body/eval_jaxpr/ppermute | solution.py:14
  305.3 5.0 collective-permute-done
  311.0 6.1 collective-permute-start
  317.2 3.7 collective-permute-done
  321.5 6.8 %collective-permute-start = (f32[8,64,128]{2,1,0:T(8,128)S(1)}, f32[8,64,128]{2,1,0:T(8,128)S(1)}, u32[]{:S(2)}, u32[]{:S(2)}) collective-permute-start(f32[8,64,128]{2,1,0:T(8,128)S(1)} %multiply_add_fusion.4), channel_id=1, source_target_pairs={{0,16},{16,32},{32,48},{48,64},{64,80},{80,96},{96,112},{112,128},... | collective-permute-start | bytes 786440 | tf_op jit(solution)/shard_map/while/body/eval_jaxpr/ppermute | solution.py:14
  328.4 3.3 collective-permute-done
  332.3 5.0 collective-permute-start
  337.3 3.3 collective-permute-done
  341.3 5.3 collective-permute-start
  346.6 3.3 collective-permute-done
  350.6 5.0 collective-permute-start
  355.7 3.3 collective-permute-done
  359.6 6.1 collective-permute-start
  369.7 6.2 collective-permute-start
  375.9 3.8 collective-permute-done
  385.2 129.7 %psum.29 = bf16[8,3,768]{2,1,0:T(4,128)(2,1)S(1)} all-reduce(f32[8,3,768]{2,1,0:T(4,128)S(1)} %reshape.508), channel_id=1, replica_groups=mesh['ctx'=32,'tp'=16] {'ctx'}, use_global_device_ids=true, to_apply=%region_14.15 | all-reduce | flops 18432 | bytes 110592 | tf_op jit(solution)/shard_map/psum | solution.py:246
  520.7 75.1 %all-reduce.6.cloned.1.call-done = f32[8,8,64,128]{3,2,1,0:T(8,128)} async-done(((f32[8,8,64,128]{3,2,1,0:T(8,128)}), f32[8,8,64,128]{3,2,1,0:T(8,128)}) %all-reduce.6.cloned.1.call-update) | async-done | bytes 2097168 | tf_op jit(solution)/shard_map/psum | solution.py:246
  602.0 28.6 %all-reduce.3 = (f32[256,1]{0,1:T(1,128)S(1)}, f32[256,1]{0,1:T(1,128)S(1)}) all-reduce(f32[256,1]{0,1:T(1,128)S(1)} %bitcast.99, f32[256,1]{0,1:T(1,128)S(1)} %bitcast.102), channel_id=1, replica_groups=mesh['ctx'=32,'tp'=16] {'tp'}, use_global_device_ids=true, to_apply=%region_5.6 | all-reduce | flops 512 | bytes 4096 | tf_op jit(solution)/shard_map/psum | solution.py:78
  (271 shorter events, 80.0 us)
Async XLA Ops:
  7.2 37.2 %copy-start.45 = (s32[64]{0:T(128)S(1)}, s32[64]{0:T(128)}, u32[]{:S(2)}) copy-start(s32[64]{0:T(128)} %param.33) | copy-start | bytes 772
  7.2 37.5 %copy-start.32 = (s32[64]{0:T(128)S(1)}, s32[64]{0:T(128)}, u32[]{:S(2)}) copy-start(s32[64]{0:T(128)} %param.35) | copy-start | bytes 772
  7.2 37.8 %copy-start.55 = (s32[64]{0:T(128)S(1)}, s32[64]{0:T(128)}, u32[]{:S(2)}) copy-start(s32[64]{0:T(128)} %param.34) | copy-start | bytes 772
  7.2 39.3 %copy-start.33 = (bf16[4,512]{1,0:T(4,128)(2,1)S(1)}, bf16[4,512]{1,0:T(4,128)(2,1)}, u32[]{:S(2)}) copy-start(bf16[4,512]{1,0:T(4,128)(2,1)} %param.27) | copy-start | bytes 12292
  7.2 39.3 %copy-start.44 = (bf16[4,256]{1,0:T(4,128)(2,1)S(1)}, bf16[4,256]{1,0:T(4,128)(2,1)}, u32[]{:S(2)}) copy-start(bf16[4,256]{1,0:T(4,128)(2,1)} %param.28) | copy-start | bytes 6148
  7.2 43.6 %copy-start.8 = (bf16[256,512]{1,0:T(8,128)(2,1)S(1)}, bf16[256,512]{1,0:T(8,128)(2,1)}, u32[]{:S(2)}) copy-start(bf16[256,512]{1,0:T(8,128)(2,1)} %param.23) | copy-start | bytes 786436
  7.2 588.5 %all-reduce.6.cloned.1.call-start = ((), (), s32[]{:S(2)}) async-start(), calls=%async_computation | async-start | bytes 4194304 | tf_op jit(solution)/shard_map/psum | solution.py:246
  8.3 42.5 %copy-start.27 = (bf16[16,256]{1,0:T(8,128)(2,1)S(1)}, bf16[16,256]{1,0:T(8,128)(2,1)}, u32[]{:S(2)}) copy-start(bf16[16,256]{1,0:T(8,128)(2,1)} %param.25) | copy-start | bytes 24580
  33.4 38.7 %copy-start.2 = (bf16[256,768]{1,0:T(8,128)(2,1)}, bf16[256,768]{1,0:T(8,128)(2,1)S(1)}, u32[]{:S(2)}) copy-start(bf16[256,768]{1,0:T(8,128)(2,1)S(1)} %constant_dynamic-update-slice_fusion.2) | copy-start | bytes 1179652
  33.5 38.7 %collective-permute-start.1 = (bf16[3,768]{1,0:T(4,128)(2,1)S(1)}, bf16[3,768]{1,0:T(4,128)(2,1)S(1)}, u32[]{:S(2)}, u32[]{:S(2)}) collective-permute-start(bf16[3,768]{1,0:T(4,128)(2,1)S(1)} %slice.119), channel_id=1, source_target_pairs={{0,16},{16,32},{32,48},{48,64},{64,80},{80,96},{96,112},{112,128},... | collective-permute-start | bytes 13832 | tf_op jit(solution)/shard_map/ppermute | solution.py:14
  75.0 8.8 %collective-permute-start = (f32[8,64,128]{2,1,0:T(8,128)S(1)}, f32[8,64,128]{2,1,0:T(8,128)S(1)}, u32[]{:S(2)}, u32[]{:S(2)}) collective-permute-start(f32[8,64,128]{2,1,0:T(8,128)S(1)} %multiply_add_fusion.4), channel_id=1, source_target_pairs={{0,16},{16,32},{32,48},{48,64},{64,80},{80,96},{96,112},{112,128},... | collective-permute-start | bytes 786440 | tf_op jit(solution)/shard_map/while/body/eval_jaxpr/ppermute | solution.py:14
  84.4 8.7 %collective-permute-start = (f32[8,64,128]{2,1,0:T(8,128)S(1)}, f32[8,64,128]{2,1,0:T(8,128)S(1)}, u32[]{:S(2)}, u32[]{:S(2)}) collective-permute-start(f32[8,64,128]{2,1,0:T(8,128)S(1)} %multiply_add_fusion.4), channel_id=1, source_target_pairs={{0,16},{16,32},{32,48},{48,64},{64,80},{80,96},{96,112},{112,128},... | collective-permute-start | bytes 786440 | tf_op jit(solution)/shard_map/while/body/eval_jaxpr/ppermute | solution.py:14
  93.9 7.8 %collective-permute-start = (f32[8,64,128]{2,1,0:T(8,128)S(1)}, f32[8,64,128]{2,1,0:T(8,128)S(1)}, u32[]{:S(2)}, u32[]{:S(2)}) collective-permute-start(f32[8,64,128]{2,1,0:T(8,128)S(1)} %multiply_add_fusion.4), channel_id=1, source_target_pairs={{0,16},{16,32},{32,48},{48,64},{64,80},{80,96},{96,112},{112,128},... | collective-permute-start | bytes 786440 | tf_op jit(solution)/shard_map/while/body/eval_jaxpr/ppermute | solution.py:14
  102.4 7.4 %collective-permute-start = (f32[8,64,128]{2,1,0:T(8,128)S(1)}, f32[8,64,128]{2,1,0:T(8,128)S(1)}, u32[]{:S(2)}, u32[]{:S(2)}) collective-permute-start(f32[8,64,128]{2,1,0:T(8,128)S(1)} %multiply_add_fusion.4), channel_id=1, source_target_pairs={{0,16},{16,32},{32,48},{48,64},{64,80},{80,96},{96,112},{112,128},... | collective-permute-start | bytes 786440 | tf_op jit(solution)/shard_map/while/body/eval_jaxpr/ppermute | solution.py:14
  110.5 7.1 %collective-permute-start = (f32[8,64,128]{2,1,0:T(8,128)S(1)}, f32[8,64,128]{2,1,0:T(8,128)S(1)}, u32[]{:S(2)}, u32[]{:S(2)}) collective-permute-start(f32[8,64,128]{2,1,0:T(8,128)S(1)} %multiply_add_fusion.4), channel_id=1, source_target_pairs={{0,16},{16,32},{32,48},{48,64},{64,80},{80,96},{96,112},{112,128},... | collective-permute-start | bytes 786440 | tf_op jit(solution)/shard_map/while/body/eval_jaxpr/ppermute | solution.py:14
  118.3 7.7 %collective-permute-start = (f32[8,64,128]{2,1,0:T(8,128)S(1)}, f32[8,64,128]{2,1,0:T(8,128)S(1)}, u32[]{:S(2)}, u32[]{:S(2)}) collective-permute-start(f32[8,64,128]{2,1,0:T(8,128)S(1)} %multiply_add_fusion.4), channel_id=1, source_target_pairs={{0,16},{16,32},{32,48},{48,64},{64,80},{80,96},{96,112},{112,128},... | collective-permute-start | bytes 786440 | tf_op jit(solution)/shard_map/while/body/eval_jaxpr/ppermute | solution.py:14
  126.8 8.6 %collective-permute-start = (f32[8,64,128]{2,1,0:T(8,128)S(1)}, f32[8,64,128]{2,1,0:T(8,128)S(1)}, u32[]{:S(2)}, u32[]{:S(2)}) collective-permute-start(f32[8,64,128]{2,1,0:T(8,128)S(1)} %multiply_add_fusion.4), channel_id=1, source_target_pairs={{0,16},{16,32},{32,48},{48,64},{64,80},{80,96},{96,112},{112,128},... | collective-permute-start | bytes 786440 | tf_op jit(solution)/shard_map/while/body/eval_jaxpr/ppermute | solution.py:14
  136.1 8.3 %collective-permute-start = (f32[8,64,128]{2,1,0:T(8,128)S(1)}, f32[8,64,128]{2,1,0:T(8,128)S(1)}, u32[]{:S(2)}, u32[]{:S(2)}) collective-permute-start(f32[8,64,128]{2,1,0:T(8,128)S(1)} %multiply_add_fusion.4), channel_id=1, source_target_pairs={{0,16},{16,32},{32,48},{48,64},{64,80},{80,96},{96,112},{112,128},... | collective-permute-start | bytes 786440 | tf_op jit(solution)/shard_map/while/body/eval_jaxpr/ppermute | solution.py:14
  145.1 9.1 %collective-permute-start = (f32[8,64,128]{2,1,0:T(8,128)S(1)}, f32[8,64,128]{2,1,0:T(8,128)S(1)}, u32[]{:S(2)}, u32[]{:S(2)}) collective-permute-start(f32[8,64,128]{2,1,0:T(8,128)S(1)} %multiply_add_fusion.4), channel_id=1, source_target_pairs={{0,16},{16,32},{32,48},{48,64},{64,80},{80,96},{96,112},{112,128},... | collective-permute-start | bytes 786440 | tf_op jit(solution)/shard_map/while/body/eval_jaxpr/ppermute | solution.py:14
  154.9 10.5 %collective-permute-start = (f32[8,64,128]{2,1,0:T(8,128)S(1)}, f32[8,64,128]{2,1,0:T(8,128)S(1)}, u32[]{:S(2)}, u32[]{:S(2)}) collective-permute-start(f32[8,64,128]{2,1,0:T(8,128)S(1)} %multiply_add_fusion.4), channel_id=1, source_target_pairs={{0,16},{16,32},{32,48},{48,64},{64,80},{80,96},{96,112},{112,128},... | collective-permute-start | bytes 786440 | tf_op jit(solution)/shard_map/while/body/eval_jaxpr/ppermute | solution.py:14
  166.1 11.9 %collective-permute-start = (f32[8,64,128]{2,1,0:T(8,128)S(1)}, f32[8,64,128]{2,1,0:T(8,128)S(1)}, u32[]{:S(2)}, u32[]{:S(2)}) collective-permute-start(f32[8,64,128]{2,1,0:T(8,128)S(1)} %multiply_add_fusion.4), channel_id=1, source_target_pairs={{0,16},{16,32},{32,48},{48,64},{64,80},{80,96},{96,112},{112,128},... | collective-permute-start | bytes 786440 | tf_op jit(solution)/shard_map/while/body/eval_jaxpr/ppermute | solution.py:14
  178.7 10.1 %collective-permute-start = (f32[8,64,128]{2,1,0:T(8,128)S(1)}, f32[8,64,128]{2,1,0:T(8,128)S(1)}, u32[]{:S(2)}, u32[]{:S(2)}) collective-permute-start(f32[8,64,128]{2,1,0:T(8,128)S(1)} %multiply_add_fusion.4), channel_id=1, source_target_pairs={{0,16},{16,32},{32,48},{48,64},{64,80},{80,96},{96,112},{112,128},... | collective-permute-start | bytes 786440 | tf_op jit(solution)/shard_map/while/body/eval_jaxpr/ppermute | solution.py:14
  189.5 8.8 %collective-permute-start = (f32[8,64,128]{2,1,0:T(8,128)S(1)}, f32[8,64,128]{2,1,0:T(8,128)S(1)}, u32[]{:S(2)}, u32[]{:S(2)}) collective-permute-start(f32[8,64,128]{2,1,0:T(8,128)S(1)} %multiply_add_fusion.4), channel_id=1, source_target_pairs={{0,16},{16,32},{32,48},{48,64},{64,80},{80,96},{96,112},{112,128},... | collective-permute-start | bytes 786440 | tf_op jit(solution)/shard_map/while/body/eval_jaxpr/ppermute | solution.py:14
  199.0 7.5 %collective-permute-start = (f32[8,64,128]{2,1,0:T(8,128)S(1)}, f32[8,64,128]{2,1,0:T(8,128)S(1)}, u32[]{:S(2)}, u32[]{:S(2)}) collective-permute-start(f32[8,64,128]{2,1,0:T(8,128)S(1)} %multiply_add_fusion.4), channel_id=1, source_target_pairs={{0,16},{16,32},{32,48},{48,64},{64,80},{80,96},{96,112},{112,128},... | collective-permute-start | bytes 786440 | tf_op jit(solution)/shard_map/while/body/eval_jaxpr/ppermute | solution.py:14
  207.2 8.6 %collective-permute-start = (f32[8,64,128]{2,1,0:T(8,128)S(1)}, f32[8,64,128]{2,1,0:T(8,128)S(1)}, u32[]{:S(2)}, u32[]{:S(2)}) collective-permute-start(f32[8,64,128]{2,1,0:T(8,128)S(1)} %multiply_add_fusion.4), channel_id=1, source_target_pairs={{0,16},{16,32},{32,48},{48,64},{64,80},{80,96},{96,112},{112,128},... | collective-permute-start | bytes 786440 | tf_op jit(solution)/shard_map/while/body/eval_jaxpr/ppermute | solution.py:14
  216.5 8.6 %collective-permute-start = (f32[8,64,128]{2,1,0:T(8,128)S(1)}, f32[8,64,128]{2,1,0:T(8,128)S(1)}, u32[]{:S(2)}, u32[]{:S(2)}) collective-permute-start(f32[8,64,128]{2,1,0:T(8,128)S(1)} %multiply_add_fusion.4), channel_id=1, source_target_pairs={{0,16},{16,32},{32,48},{48,64},{64,80},{80,96},{96,112},{112,128},... | collective-permute-start | bytes 786440 | tf_op jit(solution)/shard_map/while/body/eval_jaxpr/ppermute | solution.py:14
  225.8 8.8 %collective-permute-start = (f32[8,64,128]{2,1,0:T(8,128)S(1)}, f32[8,64,128]{2,1,0:T(8,128)S(1)}, u32[]{:S(2)}, u32[]{:S(2)}) collective-permute-start(f32[8,64,128]{2,1,0:T(8,128)S(1)} %multiply_add_fusion.4), channel_id=1, source_target_pairs={{0,16},{16,32},{32,48},{48,64},{64,80},{80,96},{96,112},{112,128},... | collective-permute-start | bytes 786440 | tf_op jit(solution)/shard_map/while/body/eval_jaxpr/ppermute | solution.py:14
  235.3 8.3 %collective-permute-start = (f32[8,64,128]{2,1,0:T(8,128)S(1)}, f32[8,64,128]{2,1,0:T(8,128)S(1)}, u32[]{:S(2)}, u32[]{:S(2)}) collective-permute-start(f32[8,64,128]{2,1,0:T(8,128)S(1)} %multiply_add_fusion.4), channel_id=1, source_target_pairs={{0,16},{16,32},{32,48},{48,64},{64,80},{80,96},{96,112},{112,128},... | collective-permute-start | bytes 786440 | tf_op jit(solution)/shard_map/while/body/eval_jaxpr/ppermute | solution.py:14
  244.3 9.4 %collective-permute-start = (f32[8,64,128]{2,1,0:T(8,128)S(1)}, f32[8,64,128]{2,1,0:T(8,128)S(1)}, u32[]{:S(2)}, u32[]{:S(2)}) collective-permute-start(f32[8,64,128]{2,1,0:T(8,128)S(1)} %multiply_add_fusion.4), channel_id=1, source_target_pairs={{0,16},{16,32},{32,48},{48,64},{64,80},{80,96},{96,112},{112,128},... | collective-permute-start | bytes 786440 | tf_op jit(solution)/shard_map/while/body/eval_jaxpr/ppermute | solution.py:14
  254.5 10.4 %collective-permute-start = (f32[8,64,128]{2,1,0:T(8,128)S(1)}, f32[8,64,128]{2,1,0:T(8,128)S(1)}, u32[]{:S(2)}, u32[]{:S(2)}) collective-permute-start(f32[8,64,128]{2,1,0:T(8,128)S(1)} %multiply_add_fusion.4), channel_id=1, source_target_pairs={{0,16},{16,32},{32,48},{48,64},{64,80},{80,96},{96,112},{112,128},... | collective-permute-start | bytes 786440 | tf_op jit(solution)/shard_map/while/body/eval_jaxpr/ppermute | solution.py:14
  265.5 10.0 %collective-permute-start = (f32[8,64,128]{2,1,0:T(8,128)S(1)}, f32[8,64,128]{2,1,0:T(8,128)S(1)}, u32[]{:S(2)}, u32[]{:S(2)}) collective-permute-start(f32[8,64,128]{2,1,0:T(8,128)S(1)} %multiply_add_fusion.4), channel_id=1, source_target_pairs={{0,16},{16,32},{32,48},{48,64},{64,80},{80,96},{96,112},{112,128},... | collective-permute-start | bytes 786440 | tf_op jit(solution)/shard_map/while/body/eval_jaxpr/ppermute | solution.py:14
  276.2 9.8 %collective-permute-start = (f32[8,64,128]{2,1,0:T(8,128)S(1)}, f32[8,64,128]{2,1,0:T(8,128)S(1)}, u32[]{:S(2)}, u32[]{:S(2)}) collective-permute-start(f32[8,64,128]{2,1,0:T(8,128)S(1)} %multiply_add_fusion.4), channel_id=1, source_target_pairs={{0,16},{16,32},{32,48},{48,64},{64,80},{80,96},{96,112},{112,128},... | collective-permute-start | bytes 786440 | tf_op jit(solution)/shard_map/while/body/eval_jaxpr/ppermute | solution.py:14
  286.7 11.0 %collective-permute-start = (f32[8,64,128]{2,1,0:T(8,128)S(1)}, f32[8,64,128]{2,1,0:T(8,128)S(1)}, u32[]{:S(2)}, u32[]{:S(2)}) collective-permute-start(f32[8,64,128]{2,1,0:T(8,128)S(1)} %multiply_add_fusion.4), channel_id=1, source_target_pairs={{0,16},{16,32},{32,48},{48,64},{64,80},{80,96},{96,112},{112,128},... | collective-permute-start | bytes 786440 | tf_op jit(solution)/shard_map/while/body/eval_jaxpr/ppermute | solution.py:14
  298.4 11.9 %collective-permute-start = (f32[8,64,128]{2,1,0:T(8,128)S(1)}, f32[8,64,128]{2,1,0:T(8,128)S(1)}, u32[]{:S(2)}, u32[]{:S(2)}) collective-permute-start(f32[8,64,128]{2,1,0:T(8,128)S(1)} %multiply_add_fusion.4), channel_id=1, source_target_pairs={{0,16},{16,32},{32,48},{48,64},{64,80},{80,96},{96,112},{112,128},... | collective-permute-start | bytes 786440 | tf_op jit(solution)/shard_map/while/body/eval_jaxpr/ppermute | solution.py:14
  311.0 9.8 %collective-permute-start = (f32[8,64,128]{2,1,0:T(8,128)S(1)}, f32[8,64,128]{2,1,0:T(8,128)S(1)}, u32[]{:S(2)}, u32[]{:S(2)}) collective-permute-start(f32[8,64,128]{2,1,0:T(8,128)S(1)} %multiply_add_fusion.4), channel_id=1, source_target_pairs={{0,16},{16,32},{32,48},{48,64},{64,80},{80,96},{96,112},{112,128},... | collective-permute-start | bytes 786440 | tf_op jit(solution)/shard_map/while/body/eval_jaxpr/ppermute | solution.py:14
  321.5 10.1 %collective-permute-start = (f32[8,64,128]{2,1,0:T(8,128)S(1)}, f32[8,64,128]{2,1,0:T(8,128)S(1)}, u32[]{:S(2)}, u32[]{:S(2)}) collective-permute-start(f32[8,64,128]{2,1,0:T(8,128)S(1)} %multiply_add_fusion.4), channel_id=1, source_target_pairs={{0,16},{16,32},{32,48},{48,64},{64,80},{80,96},{96,112},{112,128},... | collective-permute-start | bytes 786440 | tf_op jit(solution)/shard_map/while/body/eval_jaxpr/ppermute | solution.py:14
  332.3 8.2 %collective-permute-start = (f32[8,64,128]{2,1,0:T(8,128)S(1)}, f32[8,64,128]{2,1,0:T(8,128)S(1)}, u32[]{:S(2)}, u32[]{:S(2)}) collective-permute-start(f32[8,64,128]{2,1,0:T(8,128)S(1)} %multiply_add_fusion.4), channel_id=1, source_target_pairs={{0,16},{16,32},{32,48},{48,64},{64,80},{80,96},{96,112},{112,128},... | collective-permute-start | bytes 786440 | tf_op jit(solution)/shard_map/while/body/eval_jaxpr/ppermute | solution.py:14
  341.3 8.6 %collective-permute-start = (f32[8,64,128]{2,1,0:T(8,128)S(1)}, f32[8,64,128]{2,1,0:T(8,128)S(1)}, u32[]{:S(2)}, u32[]{:S(2)}) collective-permute-start(f32[8,64,128]{2,1,0:T(8,128)S(1)} %multiply_add_fusion.4), channel_id=1, source_target_pairs={{0,16},{16,32},{32,48},{48,64},{64,80},{80,96},{96,112},{112,128},... | collective-permute-start | bytes 786440 | tf_op jit(solution)/shard_map/while/body/eval_jaxpr/ppermute | solution.py:14
  350.6 8.3 %collective-permute-start = (f32[8,64,128]{2,1,0:T(8,128)S(1)}, f32[8,64,128]{2,1,0:T(8,128)S(1)}, u32[]{:S(2)}, u32[]{:S(2)}) collective-permute-start(f32[8,64,128]{2,1,0:T(8,128)S(1)} %multiply_add_fusion.4), channel_id=1, source_target_pairs={{0,16},{16,32},{32,48},{48,64},{64,80},{80,96},{96,112},{112,128},... | collective-permute-start | bytes 786440 | tf_op jit(solution)/shard_map/while/body/eval_jaxpr/ppermute | solution.py:14
  359.6 9.4 %collective-permute-start = (f32[8,64,128]{2,1,0:T(8,128)S(1)}, f32[8,64,128]{2,1,0:T(8,128)S(1)}, u32[]{:S(2)}, u32[]{:S(2)}) collective-permute-start(f32[8,64,128]{2,1,0:T(8,128)S(1)} %multiply_add_fusion.4), channel_id=1, source_target_pairs={{0,16},{16,32},{32,48},{48,64},{64,80},{80,96},{96,112},{112,128},... | collective-permute-start | bytes 786440 | tf_op jit(solution)/shard_map/while/body/eval_jaxpr/ppermute | solution.py:14
  369.7 10.0 %collective-permute-start = (f32[8,64,128]{2,1,0:T(8,128)S(1)}, f32[8,64,128]{2,1,0:T(8,128)S(1)}, u32[]{:S(2)}, u32[]{:S(2)}) collective-permute-start(f32[8,64,128]{2,1,0:T(8,128)S(1)} %multiply_add_fusion.4), channel_id=1, source_target_pairs={{0,16},{16,32},{32,48},{48,64},{64,80},{80,96},{96,112},{112,128},... | collective-permute-start | bytes 786440 | tf_op jit(solution)/shard_map/while/body/eval_jaxpr/ppermute | solution.py:14
  383.7 131.9 %copy-start.14 = (f32[768]{0:T(1024)S(1)}, f32[768]{0:T(1024)}, u32[]{:S(2)}) copy-start(f32[768]{0:T(1024)} %copy-done.13) | copy-start | bytes 9220
  383.7 131.9 %copy-start.19 = (s32[256]{0:T(256)S(1)}, s32[256]{0:T(256)}, u32[]{:S(2)}) copy-start(s32[256]{0:T(256)} %copy-done.18) | copy-start | bytes 3076
  383.7 131.9 %copy-start.35 = (s32[256]{0:T(256)S(1)}, s32[256]{0:T(256)}, u32[]{:S(2)}) copy-start(s32[256]{0:T(256)} %get-tuple-element.66) | copy-start | bytes 3076
  383.8 131.9 %copy-start.36 = (s32[6]{0:T(128)S(1)}, s32[6]{0:T(128)}, u32[]{:S(2)}) copy-start(s32[6]{0:T(128)} %get-tuple-element.73) | copy-start | bytes 76
  383.8 131.9 %copy-start.37 = (s32[6]{0:T(128)S(1)}, s32[6]{0:T(128)}, u32[]{:S(2)}) copy-start(s32[6]{0:T(128)} %get-tuple-element.74) | copy-start | bytes 76
  383.8 131.9 %copy-start.38 = (pred[6]{0:T(512)(128)(4,1)S(1)}, pred[6]{0:T(512)(128)(4,1)}, u32[]{:S(2)}) copy-start(pred[6]{0:T(512)(128)(4,1)} %broadcast_in_dim.287) | copy-start | bytes 22
  383.8 131.9 %copy-start.41 = (pred[256]{0:T(512)(128)(4,1)S(1)}, pred[256]{0:T(512)(128)(4,1)}, u32[]{:S(2)}) copy-start(pred[256]{0:T(512)(128)(4,1)} %get-tuple-element.61) | copy-start | bytes 772
  383.8 131.9 %copy-start.42 = (pred[256]{0:T(512)(128)(4,1)S(1)}, pred[256]{0:T(512)(128)(4,1)}, u32[]{:S(2)}) copy-start(pred[256]{0:T(512)(128)(4,1)} %get-tuple-element.62) | copy-start | bytes 772
  384.6 131.6 %copy-start.12 = (f32[768]{0:T(1024)S(1)}, f32[768]{0:T(1024)}, u32[]{:S(2)}) copy-start(f32[768]{0:T(1024)} %copy-done.11) | copy-start | bytes 9220
  384.6 131.6 %copy-start.34 = (s32[256]{0:T(256)S(1)}, s32[256]{0:T(256)}, u32[]{:S(2)}) copy-start(s32[256]{0:T(256)} %get-tuple-element.65) | copy-start | bytes 3076
  384.6 131.6 %copy-start.39 = (pred[256]{0:T(512)(128)(4,1)S(1)}, pred[256]{0:T(512)(128)(4,1)}, u32[]{:S(2)}) copy-start(pred[256]{0:T(512)(128)(4,1)} %get-tuple-element.59) | copy-start | bytes 772
  384.6 131.6 %copy-start.40 = (pred[256]{0:T(512)(128)(4,1)S(1)}, pred[256]{0:T(512)(128)(4,1)}, u32[]{:S(2)}) copy-start(pred[256]{0:T(512)(128)(4,1)} %get-tuple-element.60) | copy-start | bytes 772
  384.6 132.0 %copy-start.21 = (f32[768]{0:T(1024)S(1)}, f32[768]{0:T(1024)}, u32[]{:S(2)}) copy-start(f32[768]{0:T(1024)} %copy-done.20) | copy-start | bytes 9220
  384.6 132.0 %copy-start.23 = (f32[768]{0:T(1024)S(1)}, f32[768]{0:T(1024)}, u32[]{:S(2)}) copy-start(f32[768]{0:T(1024)} %copy-done.22) | copy-start | bytes 9220
  384.6 132.0 %copy-start.47 = (s32[256]{0:T(256)S(1)}, s32[256]{0:T(256)}, u32[]{:S(2)}) copy-start(s32[256]{0:T(256)} %get-tuple-element.64) | copy-start | bytes 3076
  384.7 132.0 %copy-start.52 = (pred[256]{0:T(512)(128)(4,1)S(1)}, pred[256]{0:T(512)(128)(4,1)}, u32[]{:S(2)}) copy-start(pred[256]{0:T(512)(128)(4,1)} %get-tuple-element.57) | copy-start | bytes 772
  384.7 132.0 %copy-start.53 = (pred[256]{0:T(512)(128)(4,1)S(1)}, pred[256]{0:T(512)(128)(4,1)}, u32[]{:S(2)}) copy-start(pred[256]{0:T(512)(128)(4,1)} %get-tuple-element.58) | copy-start | bytes 772
  518.2 79.9 %copy-start.49 = (pred[2]{0:T(512)(128)(4,1)S(1)}, pred[2]{0:T(512)(128)(4,1)}, u32[]{:S(2)}) copy-start(pred[2]{0:T(512)(128)(4,1)} %copy-done.48) | copy-start | bytes 10
  518.2 80.0 %copy-start.50 = (pred[256]{0:T(512)(128)(4,1)S(1)}, pred[256]{0:T(512)(128)(4,1)}, u32[]{:S(2)}) copy-start(pred[256]{0:T(512)(128)(4,1)} %broadcast_compare_fusion.2) | copy-start | bytes 772
  519.3 80.1 %copy-start.43 = (pred[256]{0:T(512)(128)(4,1)S(1)}, pred[256]{0:T(512)(128)(4,1)}, u32[]{:S(2)}) copy-start(pred[256]{0:T(512)(128)(4,1)} %get-tuple-element.45) | copy-start | bytes 772
  519.6 81.1 %copy-start.10 = (pred[256,256]{1,0:T(8,128)(4,1)S(1)}, pred[256,256]{1,0:T(8,128)(4,1)}, u32[]{:S(2)}) copy-start(pred[256,256]{1,0:T(8,128)(4,1)} %and_and_fusion) | copy-start | bytes 196612
  519.6 81.1 %copy-start.17 = (f32[8,256]{1,0:T(8,128)S(1)}, f32[8,256]{1,0:T(8,128)}, u32[]{:S(2)}) copy-start(f32[8,256]{1,0:T(8,128)} %copy-done.16) | copy-start | bytes 24580
  519.6 81.1 %copy-start.28 = (f32[8,256]{1,0:T(8,128)S(1)}, f32[8,256]{1,0:T(8,128)}, u32[]{:S(2)}) copy-start(f32[8,256]{1,0:T(8,128)} %copy.135) | copy-start | bytes 24580
  (27 other events, 315.9 us)
Sparse Core Ops, SparseCore 0:
  382.3 213.4 all-reduce.5
where the time goes:
time: 641 us; the launch traced here: 639 us
  waiting for transfers between devices  200 us (31%)
  blocking collectives  198 us (31%)
  starting transfers between devices  161 us (25%)
  other arithmetic  38.4 us (6%)
  local copies, waits for them, and re-layouts  16.2 us (3%)
  between operations  15.2 us (2%)
  matrix products  9.01 us (1%)
    ppermute x32, starting transfers between devices, passed_along(): lax.ppermute(value, axis, [(source, source + steps) for source in range(f...  161 us
    psum x1, blocking collectives, body(): all_states, all_tails = lax.psum((candidate, tail_rows), 'ctx')  130 us
    ppermute x32, waiting for transfers between devices, passed_along(): lax.ppermute(value, axis, [(source, source + steps) for source in range(f...  125 us
    psum x1, waiting for transfers between devices, body(): all_states, all_tails = lax.psum((candidate, tail_rows), 'ctx')  75.1 us
    psum x1, blocking collectives, finish(): total_squares = lax.psum(partial_squares, 'tp')  28.6 us
    all_gather x1, blocking collectives, body(): lax.all_gather(prefix_bc, 'tp', axis=0, tiled=True)  25.1 us
    add x31, other arithmetic, carry_step(): return passed_along(end_decay[:, None, None] * state + end_state, 'ctx', 1)  21.6 us
    all_gather x1, blocking collectives, body(): lax.all_gather(branch_bc, 'tp', axis=0, tiled=True)  14.8 us
  transfers between devices with their start and end apart: 33, of which 32 were waited for; matrix products, arithmetic and copies ran while one was open for 4% of the time, Pallas kernels for 0%

commit v1 on v0

--- a/solution.py
+++ b/solution.py
@@ -75,7 +75,11 @@
     mixed_out = mixed_out + skip[None, :, None] * values.astype(jnp.float32)
     gated = mixed_out.reshape(length, -1) * jax.nn.silu(gate_rows.astype(jnp.float32))
     partial_squares = jnp.sum(gated * gated, axis=1, keepdims=True)
-    total_squares = lax.psum(partial_squares, "tp")
+    total_squares = partial_squares
+    for hop in (1, 2, 4, 8):
+        total_squares = total_squares + lax.ppermute(
+            total_squares, "tp", [(dev, dev ^ hop) for dev in range(16)]
+        )
     factor = lax.rsqrt(total_squares / NORM_GROUP + EPSILON)
     return (gated * factor * gain[None, :]).astype(jnp.bfloat16)
 

time: 641 us -> 645 us (level)
  starting transfers between devices: 161 us -> 226 us
  waiting for transfers between devices: 200 us -> 167 us
  blocking collectives: 198 us -> 172 us
    ppermute x0 -> x8, starting transfers between devices: none -> 64.2 us  [finish(): lax.ppermute(total_squares, 'tp', [(dev, dev ^ hop) for dev in range(16)])]
    psum x1, waiting for transfers between devices: 75.1 us -> 37.4 us  [body(): all_states, all_tails = lax.psum((candidate, tail_rows), 'ctx')]
    psum x1 -> x0, blocking collectives: 28.6 us -> none  [finish(): total_squares = lax.psum(partial_squares, 'tp')]
  transfers between devices with their start and end apart: 33 -> 41, of which waited for: 32 -> 34; matrix products, arithmetic and copies ran while one was open for 4% -> 5% of each run, Pallas kernels for 0% -> 0%
where the time goes in v1:
time: 645 us; the launch traced here: 642 us
  starting transfers between devices  226 us (35%)
  blocking collectives  172 us (27%)
  waiting for transfers between devices  167 us (26%)
  other arithmetic  37.4 us (6%)
  local copies, waits for them, and re-layouts  15.8 us (2%)
  between operations  15.4 us (2%)
  matrix products  7.34 us (1%)
    ppermute x32, starting transfers between devices, passed_along(): lax.ppermute(value, axis, [(source, source + steps) for source in range(f...  162 us
    psum x1, blocking collectives, body(): all_states, all_tails = lax.psum((candidate, tail_rows), 'ctx')  132 us
    ppermute x32, waiting for transfers between devices, passed_along(): lax.ppermute(value, axis, [(source, source + steps) for source in range(f...  125 us
    ppermute x8, starting transfers between devices, finish(): lax.ppermute(total_squares, 'tp', [(dev, dev ^ hop) for dev in range(16)])  64.2 us
    psum x1, waiting for transfers between devices, body(): all_states, all_tails = lax.psum((candidate, tail_rows), 'ctx')  37.4 us
    all_gather x1, blocking collectives, body(): lax.all_gather(prefix_bc, 'tp', axis=0, tiled=True)  25.1 us
    add x31, other arithmetic, carry_step(): return passed_along(end_decay[:, None, None] * state + end_state, 'ctx', 1)  20.6 us
    all_gather x1, blocking collectives, body(): lax.all_gather(branch_bc, 'tp', axis=0, tiled=True)  14.8 us
  transfers between devices with their start and end apart: 41, of which 34 were waited for; matrix products, arithmetic and copies ran while one was open for 5% of the time, Pallas kernels for 0%

profile of v1, /device:TPU:1, one launch (start us, length us, event | category | flops | bytes accessed | tf_op | source)
XLA Modules:
  0.0 641.7 jit_solution(8109557423259447271)
XLA Ops:
  8.3 25.1 %all_gather.6 = bf16[256,256]{1,0:T(8,128)(2,1)S(1)} all-gather(bf16[16,256]{1,0:T(8,128)(2,1)} %param.21), channel_id=1, replica_groups=mesh['ctx'=32,'tp'=16] {'tp'}, dimensions={0}, use_global_device_ids=true | all-gather | bytes 139264 | tf_op jit(solution)/shard_map/all_gather | solution.py:201
  50.8 14.8 %all_gather.7 = bf16[256,256]{1,0:T(8,128)(2,1)S(1)} all-gather(bf16[16,256]{1,0:T(8,128)(2,1)S(1)} %copy-done.28), channel_id=1, replica_groups=mesh['ctx'=32,'tp'=16] {'tp'}, dimensions={0}, use_global_device_ids=true | all-gather | bytes 139264 | tf_op jit(solution)/shard_map/all_gather | solution.py:202
  74.3 304.6 %while.10 = (s32[]{:T(128)}, f32[8,64,128]{2,1,0:T(8,128)S(1)}, f32[8]{0:T(128)}, f32[8,64,128]{2,1,0:T(8,128)S(1)}, s32[]{:T(128)}) while((s32[]{:T(128)}, f32[8,64,128]{2,1,0:T(8,128)S(1)}, f32[8]{0:T(128)}, f32[8,64,128]{2,1,0:T(8,128)S(1)}, s32[]{:T(128)}) %tuple.49), condition=%wide.region_3.4_spmd, body=%wide.region_2.3_spmd.sunk | while | flops 131074 | bytes 1835141 | solution.py:229
  78.3 5.5 collective-permute-done
  84.4 4.1 collective-permute-start
  88.6 4.6 collective-permute-done
  93.8 4.1 collective-permute-start
  98.0 3.7 collective-permute-done
  102.3 4.1 collective-permute-start
  110.4 3.8 collective-permute-start
  114.2 3.3 collective-permute-done
  118.2 4.4 collective-permute-start
  122.6 3.3 collective-permute-done
  126.6 5.3 collective-permute-start
  131.9 3.3 collective-permute-done
  135.9 5.0 collective-permute-start
  140.9 3.3 collective-permute-done
  144.9 5.0 collective-permute-start
  149.9 4.1 collective-permute-done
  154.6 5.5 collective-permute-start
  160.1 5.1 collective-permute-done
  165.9 5.9 collective-permute-start
  171.8 5.9 collective-permute-done
  178.4 5.4 collective-permute-start
  183.8 4.7 collective-permute-done
  189.2 5.0 collective-permute-start
  194.2 3.6 collective-permute-done
  198.5 4.5 collective-permute-start
  203.0 3.3 collective-permute-done
  206.9 5.3 collective-permute-start
  216.2 5.3 collective-permute-start
  225.5 5.5 collective-permute-start
  234.9 5.0 collective-permute-start
  243.9 5.2 collective-permute-start
  249.2 4.3 collective-permute-done
  254.1 5.5 collective-permute-start
  259.6 5.2 collective-permute-done
  265.5 4.2 collective-permute-start
  269.7 6.1 collective-permute-done
  276.5 4.0 collective-permute-start
  280.5 5.3 collective-permute-done
  286.5 4.9 collective-permute-start
  291.4 5.2 collective-permute-done
  297.2 7.4 %collective-permute-start = (f32[8,64,128]{2,1,0:T(8,128)S(1)}, f32[8,64,128]{2,1,0:T(8,128)S(1)}, u32[]{:S(2)}, u32[]{:S(2)}) collective-permute-start(f32[8,64,128]{2,1,0:T(8,128)S(1)} %multiply_add_fusion.4), channel_id=1, source_target_pairs={{0,16},{16,32},{32,48},{48,64},{64,80},{80,96},{96,112},{112,128},... | collective-permute-start | bytes 786440 | tf_op jit(solution)/shard_map/while/body/eval_jaxpr/ppermute | solution.py:14
  304.7 4.9 collective-permute-done
  310.3 6.4 %collective-permute-start = (f32[8,64,128]{2,1,0:T(8,128)S(1)}, f32[8,64,128]{2,1,0:T(8,128)S(1)}, u32[]{:S(2)}, u32[]{:S(2)}) collective-permute-start(f32[8,64,128]{2,1,0:T(8,128)S(1)} %multiply_add_fusion.4), channel_id=1, source_target_pairs={{0,16},{16,32},{32,48},{48,64},{64,80},{80,96},{96,112},{112,128},... | collective-permute-start | bytes 786440 | tf_op jit(solution)/shard_map/while/body/eval_jaxpr/ppermute | solution.py:14
  316.7 3.8 collective-permute-done
  321.2 5.9 collective-permute-start
  331.0 5.3 collective-permute-start
  340.3 5.8 collective-permute-start
  350.1 5.0 collective-permute-start
  359.1 5.9 collective-permute-start
  368.9 6.2 collective-permute-start
  375.2 3.8 collective-permute-done
  384.4 33.6 %collective-permute-start.2 = (f32[256,1]{0,1:T(1,128)S(1)}, f32[256,1]{0,1:T(1,128)S(1)}, u32[]{:S(2)}, u32[]{:S(2)}) collective-permute-start(f32[256,1]{0,1:T(1,128)S(1)} %bitcast.99), channel_id=1, source_target_pairs={{0,1},{1,0},{2,3},{3,2},{4,5},{5,4},{6,7},{7,6},{8,9},{9,8},{10,11... | collective-permute-start | bytes 3080 | tf_op jit(solution)/shard_map/ppermute | solution.py:80
  418.3 132.1 %psum.14 = bf16[8,3,768]{2,1,0:T(4,128)(2,1)S(1)} all-reduce(f32[8,3,768]{2,1,0:T(4,128)S(1)} %reshape.508), channel_id=1, replica_groups=mesh['ctx'=32,'tp'=16] {'ctx'}, use_global_device_ids=true, to_apply=%region_13.14 | all-reduce | flops 18432 | bytes 110592 | tf_op jit(solution)/shard_map/psum | solution.py:250
  553.8 3.6 collective-permute-start.3
  557.4 37.4 %all-reduce.5.cloned.1.call-done = f32[8,8,64,128]{3,2,1,0:T(8,128)} async-done(((f32[8,8,64,128]{3,2,1,0:T(8,128)}), f32[8,8,64,128]{3,2,1,0:T(8,128)}) %all-reduce.5.cloned.1.call-update) | async-done | bytes 2097168 | tf_op jit(solution)/shard_map/psum | solution.py:250
  601.0 6.5 %collective-permute-start.6 = (f32[256,1]{0,1:T(1,128)S(1)}, f32[256,1]{0,1:T(1,128)S(1)}, u32[]{:S(2)}, u32[]{:S(2)}) collective-permute-start(f32[256,1]{0,1:T(1,128)S(1)} %bitcast.101), channel_id=1, source_target_pairs={{0,1},{1,0},{2,3},{3,2},{4,5},{5,4},{6,7},{7,6},{8,9},{9,8},{10,11... | collective-permute-start | bytes 3080 | tf_op jit(solution)/shard_map/ppermute | solution.py:80
  607.5 4.3 collective-permute-start.4
  611.9 3.3 collective-permute-start.7
  615.2 5.2 collective-permute-start.5
  620.5 3.4 collective-permute-start.8
  625.7 4.2 collective-permute-start.9
  (294 shorter events, 104.7 us)
Async XLA Ops:
  7.2 587.5 %all-reduce.5.cloned.1.call-start = ((), (), s32[]{:S(2)}) async-start(), calls=%async_computation | async-start | bytes 4194304 | tf_op jit(solution)/shard_map/psum | solution.py:250
  33.5 38.8 %collective-permute-start.1 = (bf16[3,768]{1,0:T(4,128)(2,1)S(1)}, bf16[3,768]{1,0:T(4,128)(2,1)S(1)}, u32[]{:S(2)}, u32[]{:S(2)}) collective-permute-start(bf16[3,768]{1,0:T(4,128)(2,1)S(1)} %slice.119), channel_id=1, source_target_pairs={{0,16},{16,32},{32,48},{48,64},{64,80},{80,96},{96,112},{112,128},... | collective-permute-start | bytes 13832 | tf_op jit(solution)/shard_map/ppermute | solution.py:14
  75.0 8.7 %collective-permute-start = (f32[8,64,128]{2,1,0:T(8,128)S(1)}, f32[8,64,128]{2,1,0:T(8,128)S(1)}, u32[]{:S(2)}, u32[]{:S(2)}) collective-permute-start(f32[8,64,128]{2,1,0:T(8,128)S(1)} %multiply_add_fusion.4), channel_id=1, source_target_pairs={{0,16},{16,32},{32,48},{48,64},{64,80},{80,96},{96,112},{112,128},... | collective-permute-start | bytes 786440 | tf_op jit(solution)/shard_map/while/body/eval_jaxpr/ppermute | solution.py:14
  84.4 8.7 %collective-permute-start = (f32[8,64,128]{2,1,0:T(8,128)S(1)}, f32[8,64,128]{2,1,0:T(8,128)S(1)}, u32[]{:S(2)}, u32[]{:S(2)}) collective-permute-start(f32[8,64,128]{2,1,0:T(8,128)S(1)} %multiply_add_fusion.4), channel_id=1, source_target_pairs={{0,16},{16,32},{32,48},{48,64},{64,80},{80,96},{96,112},{112,128},... | collective-permute-start | bytes 786440 | tf_op jit(solution)/shard_map/while/body/eval_jaxpr/ppermute | solution.py:14
  93.8 7.8 %collective-permute-start = (f32[8,64,128]{2,1,0:T(8,128)S(1)}, f32[8,64,128]{2,1,0:T(8,128)S(1)}, u32[]{:S(2)}, u32[]{:S(2)}) collective-permute-start(f32[8,64,128]{2,1,0:T(8,128)S(1)} %multiply_add_fusion.4), channel_id=1, source_target_pairs={{0,16},{16,32},{32,48},{48,64},{64,80},{80,96},{96,112},{112,128},... | collective-permute-start | bytes 786440 | tf_op jit(solution)/shard_map/while/body/eval_jaxpr/ppermute | solution.py:14
  102.3 7.4 %collective-permute-start = (f32[8,64,128]{2,1,0:T(8,128)S(1)}, f32[8,64,128]{2,1,0:T(8,128)S(1)}, u32[]{:S(2)}, u32[]{:S(2)}) collective-permute-start(f32[8,64,128]{2,1,0:T(8,128)S(1)} %multiply_add_fusion.4), channel_id=1, source_target_pairs={{0,16},{16,32},{32,48},{48,64},{64,80},{80,96},{96,112},{112,128},... | collective-permute-start | bytes 786440 | tf_op jit(solution)/shard_map/while/body/eval_jaxpr/ppermute | solution.py:14
  110.4 7.1 %collective-permute-start = (f32[8,64,128]{2,1,0:T(8,128)S(1)}, f32[8,64,128]{2,1,0:T(8,128)S(1)}, u32[]{:S(2)}, u32[]{:S(2)}) collective-permute-start(f32[8,64,128]{2,1,0:T(8,128)S(1)} %multiply_add_fusion.4), channel_id=1, source_target_pairs={{0,16},{16,32},{32,48},{48,64},{64,80},{80,96},{96,112},{112,128},... | collective-permute-start | bytes 786440 | tf_op jit(solution)/shard_map/while/body/eval_jaxpr/ppermute | solution.py:14
  118.2 7.7 %collective-permute-start = (f32[8,64,128]{2,1,0:T(8,128)S(1)}, f32[8,64,128]{2,1,0:T(8,128)S(1)}, u32[]{:S(2)}, u32[]{:S(2)}) collective-permute-start(f32[8,64,128]{2,1,0:T(8,128)S(1)} %multiply_add_fusion.4), channel_id=1, source_target_pairs={{0,16},{16,32},{32,48},{48,64},{64,80},{80,96},{96,112},{112,128},... | collective-permute-start | bytes 786440 | tf_op jit(solution)/shard_map/while/body/eval_jaxpr/ppermute | solution.py:14
  126.6 8.6 %collective-permute-start = (f32[8,64,128]{2,1,0:T(8,128)S(1)}, f32[8,64,128]{2,1,0:T(8,128)S(1)}, u32[]{:S(2)}, u32[]{:S(2)}) collective-permute-start(f32[8,64,128]{2,1,0:T(8,128)S(1)} %multiply_add_fusion.4), channel_id=1, source_target_pairs={{0,16},{16,32},{32,48},{48,64},{64,80},{80,96},{96,112},{112,128},... | collective-permute-start | bytes 786440 | tf_op jit(solution)/shard_map/while/body/eval_jaxpr/ppermute | solution.py:14
  135.9 8.3 %collective-permute-start = (f32[8,64,128]{2,1,0:T(8,128)S(1)}, f32[8,64,128]{2,1,0:T(8,128)S(1)}, u32[]{:S(2)}, u32[]{:S(2)}) collective-permute-start(f32[8,64,128]{2,1,0:T(8,128)S(1)} %multiply_add_fusion.4), channel_id=1, source_target_pairs={{0,16},{16,32},{32,48},{48,64},{64,80},{80,96},{96,112},{112,128},... | collective-permute-start | bytes 786440 | tf_op jit(solution)/shard_map/while/body/eval_jaxpr/ppermute | solution.py:14
  144.9 9.1 %collective-permute-start = (f32[8,64,128]{2,1,0:T(8,128)S(1)}, f32[8,64,128]{2,1,0:T(8,128)S(1)}, u32[]{:S(2)}, u32[]{:S(2)}) collective-permute-start(f32[8,64,128]{2,1,0:T(8,128)S(1)} %multiply_add_fusion.4), channel_id=1, source_target_pairs={{0,16},{16,32},{32,48},{48,64},{64,80},{80,96},{96,112},{112,128},... | collective-permute-start | bytes 786440 | tf_op jit(solution)/shard_map/while/body/eval_jaxpr/ppermute | solution.py:14
  154.6 10.6 %collective-permute-start = (f32[8,64,128]{2,1,0:T(8,128)S(1)}, f32[8,64,128]{2,1,0:T(8,128)S(1)}, u32[]{:S(2)}, u32[]{:S(2)}) collective-permute-start(f32[8,64,128]{2,1,0:T(8,128)S(1)} %multiply_add_fusion.4), channel_id=1, source_target_pairs={{0,16},{16,32},{32,48},{48,64},{64,80},{80,96},{96,112},{112,128},... | collective-permute-start | bytes 786440 | tf_op jit(solution)/shard_map/while/body/eval_jaxpr/ppermute | solution.py:14
  165.9 11.8 %collective-permute-start = (f32[8,64,128]{2,1,0:T(8,128)S(1)}, f32[8,64,128]{2,1,0:T(8,128)S(1)}, u32[]{:S(2)}, u32[]{:S(2)}) collective-permute-start(f32[8,64,128]{2,1,0:T(8,128)S(1)} %multiply_add_fusion.4), channel_id=1, source_target_pairs={{0,16},{16,32},{32,48},{48,64},{64,80},{80,96},{96,112},{112,128},... | collective-permute-start | bytes 786440 | tf_op jit(solution)/shard_map/while/body/eval_jaxpr/ppermute | solution.py:14
  178.4 10.1 %collective-permute-start = (f32[8,64,128]{2,1,0:T(8,128)S(1)}, f32[8,64,128]{2,1,0:T(8,128)S(1)}, u32[]{:S(2)}, u32[]{:S(2)}) collective-permute-start(f32[8,64,128]{2,1,0:T(8,128)S(1)} %multiply_add_fusion.4), channel_id=1, source_target_pairs={{0,16},{16,32},{32,48},{48,64},{64,80},{80,96},{96,112},{112,128},... | collective-permute-start | bytes 786440 | tf_op jit(solution)/shard_map/while/body/eval_jaxpr/ppermute | solution.py:14
  189.2 8.6 %collective-permute-start = (f32[8,64,128]{2,1,0:T(8,128)S(1)}, f32[8,64,128]{2,1,0:T(8,128)S(1)}, u32[]{:S(2)}, u32[]{:S(2)}) collective-permute-start(f32[8,64,128]{2,1,0:T(8,128)S(1)} %multiply_add_fusion.4), channel_id=1, source_target_pairs={{0,16},{16,32},{32,48},{48,64},{64,80},{80,96},{96,112},{112,128},... | collective-permute-start | bytes 786440 | tf_op jit(solution)/shard_map/while/body/eval_jaxpr/ppermute | solution.py:14
  198.5 7.8 %collective-permute-start = (f32[8,64,128]{2,1,0:T(8,128)S(1)}, f32[8,64,128]{2,1,0:T(8,128)S(1)}, u32[]{:S(2)}, u32[]{:S(2)}) collective-permute-start(f32[8,64,128]{2,1,0:T(8,128)S(1)} %multiply_add_fusion.4), channel_id=1, source_target_pairs={{0,16},{16,32},{32,48},{48,64},{64,80},{80,96},{96,112},{112,128},... | collective-permute-start | bytes 786440 | tf_op jit(solution)/shard_map/while/body/eval_jaxpr/ppermute | solution.py:14
  206.9 8.6 %collective-permute-start = (f32[8,64,128]{2,1,0:T(8,128)S(1)}, f32[8,64,128]{2,1,0:T(8,128)S(1)}, u32[]{:S(2)}, u32[]{:S(2)}) collective-permute-start(f32[8,64,128]{2,1,0:T(8,128)S(1)} %multiply_add_fusion.4), channel_id=1, source_target_pairs={{0,16},{16,32},{32,48},{48,64},{64,80},{80,96},{96,112},{112,128},... | collective-permute-start | bytes 786440 | tf_op jit(solution)/shard_map/while/body/eval_jaxpr/ppermute | solution.py:14
  216.2 8.6 %collective-permute-start = (f32[8,64,128]{2,1,0:T(8,128)S(1)}, f32[8,64,128]{2,1,0:T(8,128)S(1)}, u32[]{:S(2)}, u32[]{:S(2)}) collective-permute-start(f32[8,64,128]{2,1,0:T(8,128)S(1)} %multiply_add_fusion.4), channel_id=1, source_target_pairs={{0,16},{16,32},{32,48},{48,64},{64,80},{80,96},{96,112},{112,128},... | collective-permute-start | bytes 786440 | tf_op jit(solution)/shard_map/while/body/eval_jaxpr/ppermute | solution.py:14
  225.5 8.8 %collective-permute-start = (f32[8,64,128]{2,1,0:T(8,128)S(1)}, f32[8,64,128]{2,1,0:T(8,128)S(1)}, u32[]{:S(2)}, u32[]{:S(2)}) collective-permute-start(f32[8,64,128]{2,1,0:T(8,128)S(1)} %multiply_add_fusion.4), channel_id=1, source_target_pairs={{0,16},{16,32},{32,48},{48,64},{64,80},{80,96},{96,112},{112,128},... | collective-permute-start | bytes 786440 | tf_op jit(solution)/shard_map/while/body/eval_jaxpr/ppermute | solution.py:14
  234.9 8.3 %collective-permute-start = (f32[8,64,128]{2,1,0:T(8,128)S(1)}, f32[8,64,128]{2,1,0:T(8,128)S(1)}, u32[]{:S(2)}, u32[]{:S(2)}) collective-permute-start(f32[8,64,128]{2,1,0:T(8,128)S(1)} %multiply_add_fusion.4), channel_id=1, source_target_pairs={{0,16},{16,32},{32,48},{48,64},{64,80},{80,96},{96,112},{112,128},... | collective-permute-start | bytes 786440 | tf_op jit(solution)/shard_map/while/body/eval_jaxpr/ppermute | solution.py:14
  243.9 9.5 %collective-permute-start = (f32[8,64,128]{2,1,0:T(8,128)S(1)}, f32[8,64,128]{2,1,0:T(8,128)S(1)}, u32[]{:S(2)}, u32[]{:S(2)}) collective-permute-start(f32[8,64,128]{2,1,0:T(8,128)S(1)} %multiply_add_fusion.4), channel_id=1, source_target_pairs={{0,16},{16,32},{32,48},{48,64},{64,80},{80,96},{96,112},{112,128},... | collective-permute-start | bytes 786440 | tf_op jit(solution)/shard_map/while/body/eval_jaxpr/ppermute | solution.py:14
  254.1 10.8 %collective-permute-start = (f32[8,64,128]{2,1,0:T(8,128)S(1)}, f32[8,64,128]{2,1,0:T(8,128)S(1)}, u32[]{:S(2)}, u32[]{:S(2)}) collective-permute-start(f32[8,64,128]{2,1,0:T(8,128)S(1)} %multiply_add_fusion.4), channel_id=1, source_target_pairs={{0,16},{16,32},{32,48},{48,64},{64,80},{80,96},{96,112},{112,128},... | collective-permute-start | bytes 786440 | tf_op jit(solution)/shard_map/while/body/eval_jaxpr/ppermute | solution.py:14
  265.5 10.3 %collective-permute-start = (f32[8,64,128]{2,1,0:T(8,128)S(1)}, f32[8,64,128]{2,1,0:T(8,128)S(1)}, u32[]{:S(2)}, u32[]{:S(2)}) collective-permute-start(f32[8,64,128]{2,1,0:T(8,128)S(1)} %multiply_add_fusion.4), channel_id=1, source_target_pairs={{0,16},{16,32},{32,48},{48,64},{64,80},{80,96},{96,112},{112,128},... | collective-permute-start | bytes 786440 | tf_op jit(solution)/shard_map/while/body/eval_jaxpr/ppermute | solution.py:14
  276.5 9.3 %collective-permute-start = (f32[8,64,128]{2,1,0:T(8,128)S(1)}, f32[8,64,128]{2,1,0:T(8,128)S(1)}, u32[]{:S(2)}, u32[]{:S(2)}) collective-permute-start(f32[8,64,128]{2,1,0:T(8,128)S(1)} %multiply_add_fusion.4), channel_id=1, source_target_pairs={{0,16},{16,32},{32,48},{48,64},{64,80},{80,96},{96,112},{112,128},... | collective-permute-start | bytes 786440 | tf_op jit(solution)/shard_map/while/body/eval_jaxpr/ppermute | solution.py:14
  286.5 10.1 %collective-permute-start = (f32[8,64,128]{2,1,0:T(8,128)S(1)}, f32[8,64,128]{2,1,0:T(8,128)S(1)}, u32[]{:S(2)}, u32[]{:S(2)}) collective-permute-start(f32[8,64,128]{2,1,0:T(8,128)S(1)} %multiply_add_fusion.4), channel_id=1, source_target_pairs={{0,16},{16,32},{32,48},{48,64},{64,80},{80,96},{96,112},{112,128},... | collective-permute-start | bytes 786440 | tf_op jit(solution)/shard_map/while/body/eval_jaxpr/ppermute | solution.py:14
  297.2 12.4 %collective-permute-start = (f32[8,64,128]{2,1,0:T(8,128)S(1)}, f32[8,64,128]{2,1,0:T(8,128)S(1)}, u32[]{:S(2)}, u32[]{:S(2)}) collective-permute-start(f32[8,64,128]{2,1,0:T(8,128)S(1)} %multiply_add_fusion.4), channel_id=1, source_target_pairs={{0,16},{16,32},{32,48},{48,64},{64,80},{80,96},{96,112},{112,128},... | collective-permute-start | bytes 786440 | tf_op jit(solution)/shard_map/while/body/eval_jaxpr/ppermute | solution.py:14
  310.3 10.3 %collective-permute-start = (f32[8,64,128]{2,1,0:T(8,128)S(1)}, f32[8,64,128]{2,1,0:T(8,128)S(1)}, u32[]{:S(2)}, u32[]{:S(2)}) collective-permute-start(f32[8,64,128]{2,1,0:T(8,128)S(1)} %multiply_add_fusion.4), channel_id=1, source_target_pairs={{0,16},{16,32},{32,48},{48,64},{64,80},{80,96},{96,112},{112,128},... | collective-permute-start | bytes 786440 | tf_op jit(solution)/shard_map/while/body/eval_jaxpr/ppermute | solution.py:14
  321.2 9.1 %collective-permute-start = (f32[8,64,128]{2,1,0:T(8,128)S(1)}, f32[8,64,128]{2,1,0:T(8,128)S(1)}, u32[]{:S(2)}, u32[]{:S(2)}) collective-permute-start(f32[8,64,128]{2,1,0:T(8,128)S(1)} %multiply_add_fusion.4), channel_id=1, source_target_pairs={{0,16},{16,32},{32,48},{48,64},{64,80},{80,96},{96,112},{112,128},... | collective-permute-start | bytes 786440 | tf_op jit(solution)/shard_map/while/body/eval_jaxpr/ppermute | solution.py:14
  331.0 8.6 %collective-permute-start = (f32[8,64,128]{2,1,0:T(8,128)S(1)}, f32[8,64,128]{2,1,0:T(8,128)S(1)}, u32[]{:S(2)}, u32[]{:S(2)}) collective-permute-start(f32[8,64,128]{2,1,0:T(8,128)S(1)} %multiply_add_fusion.4), channel_id=1, source_target_pairs={{0,16},{16,32},{32,48},{48,64},{64,80},{80,96},{96,112},{112,128},... | collective-permute-start | bytes 786440 | tf_op jit(solution)/shard_map/while/body/eval_jaxpr/ppermute | solution.py:14
  340.3 9.1 %collective-permute-start = (f32[8,64,128]{2,1,0:T(8,128)S(1)}, f32[8,64,128]{2,1,0:T(8,128)S(1)}, u32[]{:S(2)}, u32[]{:S(2)}) collective-permute-start(f32[8,64,128]{2,1,0:T(8,128)S(1)} %multiply_add_fusion.4), channel_id=1, source_target_pairs={{0,16},{16,32},{32,48},{48,64},{64,80},{80,96},{96,112},{112,128},... | collective-permute-start | bytes 786440 | tf_op jit(solution)/shard_map/while/body/eval_jaxpr/ppermute | solution.py:14
  350.1 8.3 %collective-permute-start = (f32[8,64,128]{2,1,0:T(8,128)S(1)}, f32[8,64,128]{2,1,0:T(8,128)S(1)}, u32[]{:S(2)}, u32[]{:S(2)}) collective-permute-start(f32[8,64,128]{2,1,0:T(8,128)S(1)} %multiply_add_fusion.4), channel_id=1, source_target_pairs={{0,16},{16,32},{32,48},{48,64},{64,80},{80,96},{96,112},{112,128},... | collective-permute-start | bytes 786440 | tf_op jit(solution)/shard_map/while/body/eval_jaxpr/ppermute | solution.py:14
  359.1 9.2 %collective-permute-start = (f32[8,64,128]{2,1,0:T(8,128)S(1)}, f32[8,64,128]{2,1,0:T(8,128)S(1)}, u32[]{:S(2)}, u32[]{:S(2)}) collective-permute-start(f32[8,64,128]{2,1,0:T(8,128)S(1)} %multiply_add_fusion.4), channel_id=1, source_target_pairs={{0,16},{16,32},{32,48},{48,64},{64,80},{80,96},{96,112},{112,128},... | collective-permute-start | bytes 786440 | tf_op jit(solution)/shard_map/while/body/eval_jaxpr/ppermute | solution.py:14
  368.9 10.1 %collective-permute-start = (f32[8,64,128]{2,1,0:T(8,128)S(1)}, f32[8,64,128]{2,1,0:T(8,128)S(1)}, u32[]{:S(2)}, u32[]{:S(2)}) collective-permute-start(f32[8,64,128]{2,1,0:T(8,128)S(1)} %multiply_add_fusion.4), channel_id=1, source_target_pairs={{0,16},{16,32},{32,48},{48,64},{64,80},{80,96},{96,112},{112,128},... | collective-permute-start | bytes 786440 | tf_op jit(solution)/shard_map/while/body/eval_jaxpr/ppermute | solution.py:14
  383.7 167.3 %copy-start.15 = (f32[768]{0:T(1024)S(1)}, f32[768]{0:T(1024)}, u32[]{:S(2)}) copy-start(f32[768]{0:T(1024)} %copy-done.14) | copy-start | bytes 9220
  383.7 167.3 %copy-start.20 = (s32[256]{0:T(256)S(1)}, s32[256]{0:T(256)}, u32[]{:S(2)}) copy-start(s32[256]{0:T(256)} %copy-done.19) | copy-start | bytes 3076
  383.7 167.3 %copy-start.36 = (s32[256]{0:T(256)S(1)}, s32[256]{0:T(256)}, u32[]{:S(2)}) copy-start(s32[256]{0:T(256)} %get-tuple-element.64) | copy-start | bytes 3076
  383.8 167.3 %copy-start.37 = (s32[6]{0:T(128)S(1)}, s32[6]{0:T(128)}, u32[]{:S(2)}) copy-start(s32[6]{0:T(128)} %get-tuple-element.71) | copy-start | bytes 76
  383.8 167.3 %copy-start.38 = (s32[6]{0:T(128)S(1)}, s32[6]{0:T(128)}, u32[]{:S(2)}) copy-start(s32[6]{0:T(128)} %get-tuple-element.72) | copy-start | bytes 76
  383.8 167.3 %copy-start.39 = (pred[6]{0:T(512)(128)(4,1)S(1)}, pred[6]{0:T(512)(128)(4,1)}, u32[]{:S(2)}) copy-start(pred[6]{0:T(512)(128)(4,1)} %broadcast_in_dim.287) | copy-start | bytes 22
  383.8 167.3 %copy-start.42 = (pred[256]{0:T(512)(128)(4,1)S(1)}, pred[256]{0:T(512)(128)(4,1)}, u32[]{:S(2)}) copy-start(pred[256]{0:T(512)(128)(4,1)} %get-tuple-element.59) | copy-start | bytes 772
  383.8 167.3 %copy-start.43 = (pred[256]{0:T(512)(128)(4,1)S(1)}, pred[256]{0:T(512)(128)(4,1)}, u32[]{:S(2)}) copy-start(pred[256]{0:T(512)(128)(4,1)} %get-tuple-element.60) | copy-start | bytes 772
  383.8 167.7 %copy-start.13 = (f32[768]{0:T(1024)S(1)}, f32[768]{0:T(1024)}, u32[]{:S(2)}) copy-start(f32[768]{0:T(1024)} %copy-done.12) | copy-start | bytes 9220
  383.8 167.7 %copy-start.35 = (s32[256]{0:T(256)S(1)}, s32[256]{0:T(256)}, u32[]{:S(2)}) copy-start(s32[256]{0:T(256)} %get-tuple-element.63) | copy-start | bytes 3076
  383.8 167.7 %copy-start.40 = (pred[256]{0:T(512)(128)(4,1)S(1)}, pred[256]{0:T(512)(128)(4,1)}, u32[]{:S(2)}) copy-start(pred[256]{0:T(512)(128)(4,1)} %get-tuple-element.57) | copy-start | bytes 772
  383.8 167.7 %copy-start.41 = (pred[256]{0:T(512)(128)(4,1)S(1)}, pred[256]{0:T(512)(128)(4,1)}, u32[]{:S(2)}) copy-start(pred[256]{0:T(512)(128)(4,1)} %get-tuple-element.58) | copy-start | bytes 772
  384.1 168.0 %copy-start.22 = (f32[768]{0:T(1024)S(1)}, f32[768]{0:T(1024)}, u32[]{:S(2)}) copy-start(f32[768]{0:T(1024)} %copy-done.21) | copy-start | bytes 9220
  384.1 168.0 %copy-start.24 = (f32[768]{0:T(1024)S(1)}, f32[768]{0:T(1024)}, u32[]{:S(2)}) copy-start(f32[768]{0:T(1024)} %copy-done.23) | copy-start | bytes 9220
  384.1 168.0 %copy-start.48 = (s32[256]{0:T(256)S(1)}, s32[256]{0:T(256)}, u32[]{:S(2)}) copy-start(s32[256]{0:T(256)} %get-tuple-element.62) | copy-start | bytes 3076
  384.1 168.0 %copy-start.53 = (pred[256]{0:T(512)(128)(4,1)S(1)}, pred[256]{0:T(512)(128)(4,1)}, u32[]{:S(2)}) copy-start(pred[256]{0:T(512)(128)(4,1)} %get-tuple-element.55) | copy-start | bytes 772
  384.1 168.0 %copy-start.54 = (pred[256]{0:T(512)(128)(4,1)S(1)}, pred[256]{0:T(512)(128)(4,1)}, u32[]{:S(2)}) copy-start(pred[256]{0:T(512)(128)(4,1)} %get-tuple-element.56) | copy-start | bytes 772
  384.4 169.4 %collective-permute-start.2 = (f32[256,1]{0,1:T(1,128)S(1)}, f32[256,1]{0,1:T(1,128)S(1)}, u32[]{:S(2)}, u32[]{:S(2)}) collective-permute-start(f32[256,1]{0,1:T(1,128)S(1)} %bitcast.99), channel_id=1, source_target_pairs={{0,1},{1,0},{2,3},{3,2},{4,5},{5,4},{6,7},{7,6},{8,9},{9,8},{10,11... | collective-permute-start | bytes 3080 | tf_op jit(solution)/shard_map/ppermute | solution.py:80
  552.8 44.2 %copy-start.50 = (pred[2]{0:T(512)(128)(4,1)S(1)}, pred[2]{0:T(512)(128)(4,1)}, u32[]{:S(2)}) copy-start(pred[2]{0:T(512)(128)(4,1)} %copy-done.49) | copy-start | bytes 10
  552.8 44.3 %copy-start.51 = (pred[256]{0:T(512)(128)(4,1)S(1)}, pred[256]{0:T(512)(128)(4,1)}, u32[]{:S(2)}) copy-start(pred[256]{0:T(512)(128)(4,1)} %broadcast_compare_fusion.2) | copy-start | bytes 772
  553.6 44.9 %copy-start.44 = (pred[256]{0:T(512)(128)(4,1)S(1)}, pred[256]{0:T(512)(128)(4,1)}, u32[]{:S(2)}) copy-start(pred[256]{0:T(512)(128)(4,1)} %get-tuple-element.43) | copy-start | bytes 772
  553.6 46.1 %copy-start.11 = (pred[256,256]{1,0:T(8,128)(4,1)S(1)}, pred[256,256]{1,0:T(8,128)(4,1)}, u32[]{:S(2)}) copy-start(pred[256,256]{1,0:T(8,128)(4,1)} %and_and_fusion) | copy-start | bytes 196612
  553.6 46.1 %copy-start.18 = (f32[8,256]{1,0:T(8,128)S(1)}, f32[8,256]{1,0:T(8,128)}, u32[]{:S(2)}) copy-start(f32[8,256]{1,0:T(8,128)} %copy-done.17) | copy-start | bytes 24580
  553.6 46.1 %copy-start.29 = (f32[8,256]{1,0:T(8,128)S(1)}, f32[8,256]{1,0:T(8,128)}, u32[]{:S(2)}) copy-start(f32[8,256]{1,0:T(8,128)} %copy.135) | copy-start | bytes 24580
  553.8 53.7 %collective-permute-start.3 = (f32[256,1]{0,1:T(1,128)S(1)}, f32[256,1]{0,1:T(1,128)S(1)}, u32[]{:S(2)}, u32[]{:S(2)}) collective-permute-start(f32[256,1]{0,1:T(1,128)S(1)} %add.270), channel_id=1, source_target_pairs={{0,2},{1,3},{2,0},{3,1},{4,6},{5,7},{6,4},{7,5},{8,10},{9,11},{10,... | collective-permute-start | bytes 3080 | tf_op jit(solution)/shard_map/ppermute | solution.py:80
  601.0 10.9 %collective-permute-start.6 = (f32[256,1]{0,1:T(1,128)S(1)}, f32[256,1]{0,1:T(1,128)S(1)}, u32[]{:S(2)}, u32[]{:S(2)}) collective-permute-start(f32[256,1]{0,1:T(1,128)S(1)} %bitcast.101), channel_id=1, source_target_pairs={{0,1},{1,0},{2,3},{3,2},{4,5},{5,4},{6,7},{7,6},{8,9},{9,8},{10,11... | collective-permute-start | bytes 3080 | tf_op jit(solution)/shard_map/ppermute | solution.py:80
  607.5 7.7 %collective-permute-start.4 = (f32[256,1]{0,1:T(1,128)S(1)}, f32[256,1]{0,1:T(1,128)S(1)}, u32[]{:S(2)}, u32[]{:S(2)}) collective-permute-start(f32[256,1]{0,1:T(1,128)S(1)} %add.271), channel_id=1, source_target_pairs={{0,4},{1,5},{2,6},{3,7},{4,0},{5,1},{6,2},{7,3},{8,12},{9,13},{10,... | collective-permute-start | bytes 3080 | tf_op jit(solution)/shard_map/ppermute | solution.py:80
  611.9 8.6 %collective-permute-start.7 = (f32[256,1]{0,1:T(1,128)S(1)}, f32[256,1]{0,1:T(1,128)S(1)}, u32[]{:S(2)}, u32[]{:S(2)}) collective-permute-start(f32[256,1]{0,1:T(1,128)S(1)} %add.305), channel_id=1, source_target_pairs={{0,2},{1,3},{2,0},{3,1},{4,6},{5,7},{6,4},{7,5},{8,10},{9,11},{10,... | collective-permute-start | bytes 3080 | tf_op jit(solution)/shard_map/ppermute | solution.py:80
  615.2 8.7 %collective-permute-start.5 = (f32[256,1]{0,1:T(1,128)S(1)}, f32[256,1]{0,1:T(1,128)S(1)}, u32[]{:S(2)}, u32[]{:S(2)}) collective-permute-start(f32[256,1]{0,1:T(1,128)S(1)} %add.272), channel_id=1, source_target_pairs={{0,8},{1,9},{2,10},{3,11},{4,12},{5,13},{6,14},{7,15},{8,0},{9,1},... | collective-permute-start | bytes 3080 | tf_op jit(solution)/shard_map/ppermute | solution.py:80
  620.5 5.2 collective-permute-start.8
  625.7 8.2 %collective-permute-start.9 = (f32[256,1]{0,1:T(1,128)S(1)}, f32[256,1]{0,1:T(1,128)S(1)}, u32[]{:S(2)}, u32[]{:S(2)}) collective-permute-start(f32[256,1]{0,1:T(1,128)S(1)} %add.307), channel_id=1, source_target_pairs={{0,8},{1,9},{2,10},{3,11},{4,12},{5,13},{6,14},{7,15},{8,0},{9,1},... | collective-permute-start | bytes 3080 | tf_op jit(solution)/shard_map/ppermute | solution.py:80
  (36 other events, 771.0 us)
Sparse Core Ops, SparseCore 0:
  381.5 213.2 all-reduce.4
